TPU v7x, 32 devices: a whole 2x2x4 slice. The times are simulated.
32 devices in a mesh: space: 8 (over z, x), ray: 4 (over y, core).
Axes of the slice: x: 2, y: 2, z: 4, core: 2. Of those that a mesh axis runs over, the one named last changes fastest.
Arguments:
- excite: float32 [2, 16384], P(None, ('space', 'ray')), may hold values from -6 to 6
- history: float32 [64, 16384], P(None, ('space', 'ray')), may hold values from -6 to 6
- near_mats: float32 [128, 8, 3, 128, 128], P(('space', 'ray')), may hold values from -0.109375 to 0.109375
- neighbours: int32 [128, 8], P(('space', 'ray')), may hold values from 0 to 127, as said below
- self_inverse: float32 [128, 128, 128], P(('space', 'ray')), may hold values from -3 to 4
- radiation: float32 [128, 8192, 128], P(('space', 'ray')), may hold values from -0.1875 to 0.1875
- directions: float32 [3, 8192], replicated, may hold values from -1 to 1, as said below
- centers: float32 [3, 8], replicated, may hold values from -1 to 16, as said below
- counts: int32 [128], P(('space', 'ray')), may hold values from 32 to 128
Outputs:
- currents: float32 [2, 16384], P(None, ('space', 'ray'))
Inputs may be any that keep to these rules, and one draw needn't show every extreme that they name: `neighbours`: every neighbour is a box within 4 boxes of its row's box. `directions`: each column is a unit vector. `centers`: the first coordinate of column c lies within 0.4 of 2 c, the others within -1 and 1.
All inputs are finite; a program needn't handle non-finite values.
Results may differ from a plain program's by a relative error of at most 0.0003.
Values sent between devices are 32-bit elements; how exact they have to be, the bound alone decides.
A program may use at most 128 MiB of HBM per device.

v0:
```python
import functools
import math

import jax
import jax.numpy as jnp
import numpy as np
from jax import lax
from jax.experimental import pallas as pl
from jax.experimental.pallas import tpu as pltpu
from jax.sharding import PartitionSpec as P

TAU = 48
KN = 3
BLOCK = 512
MESH = pl.DeviceIdType.MESH
EXACT = lax.Precision.HIGHEST
F32 = jnp.float32
BF16 = jnp.bfloat16


def dot_nt(a, b, precision=None):
    return lax.dot_general(a, b, (((1,), (1,)), ((), ())), precision=precision, preferred_element_type=F32)


def split(x):
    hi = x.astype(BF16)
    return hi, (x - hi.astype(F32)).astype(BF16)


def stacked(x):
    hi, lo = split(x)
    return jnp.concatenate([hi, lo], axis=0)


def clenshaw(row, twice, shape):
    later, latest = jnp.zeros(shape, F32), jnp.zeros(shape, F32)
    for m in reversed(range(TAU)):
        later, latest = row(m) + twice * later - latest, later
    return later - latest


def kernel(
    ns, nr, first_column,
    excite, history, basis, directions, centers, counts, neighbours, near_hbm, inv_hbm, rad_hbm,
    out,
    rad, rh, rl, near, inv, window, cwindow, twice, weight, ochunk, y1, y2, e0, p2, got1, send2, got2, samp,
    near1, near2, cur,
    rad_sem, near_sem, inv_sem, win_s, win_r, s1, r1, s2, r2, s3, r3,
):
    boxes, pb = near_hbm.shape[0], near_hbm.shape[-1]
    slots = near_hbm.shape[1]
    length = history.shape[0]
    rq = rad.shape[2]
    db = ochunk.shape[1]
    c, r = lax.axis_index("space"), lax.axis_index("ray")
    lin = c * nr + r
    total = ns * nr
    norm = math.sqrt(2.0 / length)

    def place(b, j):
        return jnp.clip(neighbours[b, j] - lin * boxes + boxes, 0, 3 * boxes - 1)

    def quarter(i):
        return (r + 1 + i) % nr

    loads = []
    for i in range(nr):
        start = pl.multiple_of(quarter(i) * rq, rq)
        load = pltpu.make_async_copy(rad_hbm.at[:, pl.ds(start, rq), :], rad.at[i], rad_sem.at[i])
        load.start()
        loads.append(load)
    near_load = pltpu.make_async_copy(near_hbm, near, near_sem)
    near_load.start()
    inv_load = pltpu.make_async_copy(inv_hbm, inv, inv_sem)
    inv_load.start()

    right, left = (lin + 1) % total, (lin + total - 1) % total
    right_id, left_id = (right // nr, right % nr), (left // nr, left % nr)
    barrier = pltpu.get_barrier_semaphore()
    peers = [(c, (r + o) % nr) for o in range(1, nr)] + [((c + o) % ns, r) for o in range(1, ns)]
    peers += [right_id, left_id]
    for peer in peers:
        pl.semaphore_signal(barrier, inc=1, device_id=peer, device_id_type=MESH)

    row_ids = lax.broadcasted_iota(jnp.int32, (ns, 128), 0)
    seps = []
    for x in range(3):
        column = jnp.zeros((ns, 128), F32)
        for s in range(ns):
            column = jnp.where(row_ids == s, centers[x, s], column)
        seps.append(column - centers[x, c])
    distant = jnp.abs(row_ids - c) >= 2
    distance = jnp.sqrt(seps[0] * seps[0] + seps[1] * seps[1] + seps[2] * seps[2])
    distance = jnp.where(distant, distance, 1.0)
    half_gain = jnp.where(distant, 0.5 / distance, 0.0)
    reach = 2.0 * ns + 4.0
    for i in range(nr):

        @pl.loop(0, rq // db)
        def _(j, i=i):
            here = pl.ds(pl.multiple_of(j * db, db), db)
            there = pl.ds(pl.multiple_of(quarter(i) * rq + j * db, db), db)
            along = jnp.zeros((ns, db), F32)
            for x in range(3):
                along = along + directions[x : x + 1, there] * seps[x][:, :1]
            half = (math.pi * (0.5 * length + 0.5) / length + along * (math.pi * 0.375 / reach)) * 0.5
            ch = jnp.cos(half)
            twice[i, :, here] = 4.0 * ch * ch - 2.0
            weight[i, :, here] = half_gain[:, :1] * (1.0 + along / distance[:, :1]) * (ch * norm)

    x1 = stacked(jnp.dot(basis[...], history[...], precision=EXACT, preferred_element_type=F32))
    for b in range(boxes):
        window[boxes + b] = history[0:8, b * pb : (b + 1) * pb]

    pl.semaphore_wait(barrier, len(peers))
    sent = []

    def send(src, dst, ssem, rsem, target):
        copy = pltpu.make_async_remote_copy(
            src_ref=src, dst_ref=dst, send_sem=ssem, recv_sem=rsem, device_id=target, device_id_type=MESH
        )
        copy.start()
        sent.append(copy)
        return copy

    def exchange(ref, t):
        mine = ref.at[pl.ds(boxes, boxes)]
        return [
            send(mine, ref.at[pl.ds(0, boxes)], win_s.at[t, 0], win_r.at[t, 0], right_id),
            send(mine, ref.at[pl.ds(2 * boxes, boxes)], win_s.at[t, 1], win_r.at[t, 1], left_id),
        ]

    def scatter(src, t, i):
        return send(src.at[i], got1.at[t, i], s1.at[t, i], r1.at[t, i], (c, quarter(i)))

    def translate(src, t, copies):
        for copy in copies:
            copy.wait_recv()
        reduced = src[nr - 1]
        for i in range(nr - 1):
            reduced = reduced + got1[t, i]
        for s in range(ns):
            send2[t, s] = reduced[s : s + 1, :]
        return [
            send(send2.at[t, (c + o) % ns], got2.at[t, o - 1], s2.at[t, o - 1], r2.at[t, o - 1], ((c + o) % ns, r))
            for o in range(1, ns)
        ]

    def collect(t, copies):
        for copy in copies:
            copy.wait_recv()
        value = got2[t, 0]
        for o in range(1, ns - 1):
            value = value + got2[t, o]
        samp[t, nr - 1] = value
        return [
            send(samp.at[t, nr - 1], samp.at[t, nr - 1 - o], s3.at[t, o - 1], r3.at[t, o - 1], (c, (r + o) % nr))
            for o in range(1, nr)
        ]

    def far_part(t, i):
        s = stacked(jnp.broadcast_to(samp[t, i], (8, rq)))
        top = jnp.dot(s, rh[i], preferred_element_type=F32)
        low = jnp.dot(s[:8], rl[i], preferred_element_type=F32)
        return top[:8] + top[8:] + low

    def solve(t, copies, near_ref):
        far = far_part(t, nr - 1)
        for copy in copies:
            copy.wait_recv()
        for i in range(nr - 1):
            far = far + far_part(t, i)
        lanes = lax.broadcasted_iota(jnp.int32, (8, pb), 1)
        for b in range(boxes):
            cols = slice(b * pb, (b + 1) * pb)
            rhs = excite[t : t + 1, cols] - near_ref[b] - far[:, cols]
            value = jnp.where(lanes < counts[b], dot_nt(rhs, inv[b], EXACT), 0.0)
            cur[b] = value
            out[t : t + 1, cols] = value[:1]

    win_copies = exchange(window, 0)

    copies = []
    for i in range(nr):
        loads[i].wait()

        @pl.loop(0, rq // db)
        def _(j, i=i):
            here = pl.ds(pl.multiple_of(j * db, db), db)
            x = jnp.concatenate([rad[i, b, here, :] for b in range(boxes)], axis=1)
            hi, lo = split(x)
            rh[i, here, :] = hi
            rl[i, here, :] = lo
            both = dot_nt(x1, hi)
            value = both[: 2 * TAU] + both[2 * TAU :] + dot_nt(x1[: 2 * TAU], lo)
            ochunk[...] = value[:TAU]
            p2[i, :, here] = value[TAU:]
            y1[i, :, here] = weight[i, :, here] * clenshaw(
                lambda m: ochunk[m : m + 1, :], twice[i, :, here], (ns, db)
            )

        if i < nr - 1:
            copies.append(scatter(y1, 0, i))

    def later_part(i):
        @pl.loop(0, rq // db)
        def _(j):
            here = pl.ds(pl.multiple_of(j * db, db), db)
            w, c2 = weight[i, :, here], twice[i, :, here]
            y2[i, :, here] = w * clenshaw(lambda m: p2[i, m : m + 1, here], c2, (ns, db))
            e0[i, :, here] = w * clenshaw(lambda m: first_column[m], c2, (ns, db))

    def near_part():
        near_load.wait()
        for copy in win_copies:
            copy.wait_recv()
        ones = jnp.ones((8, pb), F32)

        @pl.loop(0, boxes)
        def _(b):
            now, later = jnp.zeros((pb, pb), F32), jnp.zeros((pb, pb), F32)
            for j in range(slots):
                rows = window[place(b, j)]
                for k in range(KN):
                    mat = near[b, j, k]
                    now = now + mat * rows[k : k + 1]
                    if k:
                        later = later + mat * rows[k - 1 : k]
            near1[b] = dot_nt(ones, now, EXACT)
            near2[b] = dot_nt(ones, later, EXACT)

    near_part()
    copies = translate(y1, 0, copies)
    for i in range(nr // 2):
        later_part(i)
    copies = collect(0, copies)
    for i in range(nr // 2, nr):
        later_part(i)
    inv_load.wait()
    solve(0, copies, near1)

    for b in range(boxes):
        cwindow[boxes + b] = cur[b]
    win_copies = exchange(cwindow, 1)
    xc = stacked(jnp.concatenate([cur[b] for b in range(boxes)], axis=1))
    copies = []
    for i in range(nr):

        @pl.loop(0, rq // db)
        def _(j, i=i):
            here = pl.ds(pl.multiple_of(j * db, db), db)
            top = dot_nt(xc, rh[i, here, :])
            low = dot_nt(xc[:8], rl[i, here, :])
            value = (top[:8] + top[8:] + low)[:1]
            y2[i, :, here] = y2[i, :, here] + e0[i, :, here] * value

        if i < nr - 1:
            copies.append(scatter(y2, 1, i))
    for copy in win_copies:
        copy.wait_recv()
    ones = jnp.ones((8, pb), F32)

    @pl.loop(0, boxes)
    def _(b):
        now = jnp.zeros((pb, pb), F32)
        for j in range(slots):
            now = now + near[b, j, 0] * cwindow[place(b, j)][:1]
        near2[b] = near2[b] + dot_nt(ones, now, EXACT)

    copies = translate(y2, 1, copies)
    copies = collect(1, copies)
    solve(1, copies, near2)
    for copy in sent:
        copy.wait_send()


def local(ns, nr, excite, history, near_mats, neighbours, self_inverse, radiation, directions, centers, counts):
    boxes, rays, pb = radiation.shape
    length = history.shape[0]
    steps = excite.shape[0]
    rq = rays // nr
    db = min(BLOCK, rq)
    patches = boxes * pb
    orders, times = np.arange(TAU)[:, None] + 0.5, np.arange(length)[None, :] + 0.5
    basis = np.sqrt(2.0 / length) * np.cos(np.pi * orders * times / length)
    shifted = np.concatenate([basis[:, 1:], np.zeros((TAU, 1))], axis=1)
    first_column = [float(v) for v in basis[:, 0]]
    both = jnp.asarray(np.concatenate([basis, shifted], axis=0), F32)
    vmem = pl.BlockSpec(memory_space=pltpu.VMEM)
    smem = pl.BlockSpec(memory_space=pltpu.SMEM)
    hbm = pl.BlockSpec(memory_space=pl.ANY)
    dma = pltpu.SemaphoreType.DMA
    return pl.pallas_call(
        functools.partial(kernel, ns, nr, first_column),
        out_shape=jax.ShapeDtypeStruct((steps, patches), F32),
        in_specs=[vmem] * 4 + [smem] * 3 + [hbm] * 3,
        out_specs=vmem,
        scratch_shapes=[
            pltpu.VMEM((nr, boxes, rq, pb), F32),
            pltpu.VMEM((nr, rq, patches), BF16),
            pltpu.VMEM((nr, rq, patches), BF16),
            pltpu.VMEM(near_mats.shape, F32),
            pltpu.VMEM(self_inverse.shape, F32),
            pltpu.VMEM((3 * boxes, 8, pb), F32),
            pltpu.VMEM((3 * boxes, 8, pb), F32),
            pltpu.VMEM((nr, ns, rq), F32),
            pltpu.VMEM((nr, ns, rq), F32),
            pltpu.VMEM((TAU, db), F32),
            pltpu.VMEM((nr, ns, rq), F32),
            pltpu.VMEM((nr, ns, rq), F32),
            pltpu.VMEM((nr, ns, rq), F32),
            pltpu.VMEM((nr, TAU, rq), F32),
            pltpu.VMEM((steps, nr - 1, ns, rq), F32),
            pltpu.VMEM((steps, ns, 1, rq), F32),
            pltpu.VMEM((steps, ns - 1, 1, rq), F32),
            pltpu.VMEM((steps, nr, 1, rq), F32),
            pltpu.VMEM((boxes, 8, pb), F32),
            pltpu.VMEM((boxes, 8, pb), F32),
            pltpu.VMEM((boxes, 8, pb), F32),
            dma((nr,)), dma(()), dma(()),
            dma((steps, 2)), dma((steps, 2)),
            dma((steps, nr - 1)), dma((steps, nr - 1)),
            dma((steps, ns - 1)), dma((steps, ns - 1)),
            dma((steps, nr - 1)), dma((steps, nr - 1)),
        ],
        compiler_params=pltpu.CompilerParams(
            collective_id=0, has_side_effects=True, vmem_limit_bytes=58 * 1024 * 1024
        ),
    )(excite, history, both, directions, centers, counts, neighbours, near_mats, self_inverse, radiation)


def solution(mesh):
    placed = (
        P(None, ("space", "ray")),
        P(None, ("space", "ray")),
        P(("space", "ray"), None, None, None, None),
        P(("space", "ray"), None),
        P(("space", "ray"), None, None),
        P(("space", "ray"), None, None),
        P(),
        P(),
        P(("space", "ray")),
    )
    return jax.shard_map(
        functools.partial(local, mesh.shape["space"], mesh.shape["ray"]),
        mesh=mesh,
        in_specs=placed,
        out_specs=P(None, ("space", "ray")),
        check_vma=False,
    )
```

profile of v0, /device:TPU:0, one launch (start us, length us, event | category | flops | bytes accessed | tf_op | source)
XLA Modules:
  0.0 47.6 jit_solution(8418668963353929181)
XLA Ops:
  0.0 46.3 %shard_map.100 = f32[2,512]{1,0:T(2,128)} custom-call(f32[2,512]{1,0:T(2,128)} %excite.1, f32[64,512]{1,0:T(8,128)} %history.1, f32[96,64]{1,0:T(8,128)} %constant.2.clone.basis, f32[3,8192]{1,0:T(4,128)} %directions.1, f32[3,8]{1,0:T(4,128)} %centers.1, s32[4]{0:T(128)} %counts.1, s32[4,8]{1,0:T(4,128)} %neighbours.1, f32[4,8,3,128,128]{4,3,2,1,0:T(8,128)} %near_hbm.1, ...), custom_call_target="tpu_custom_call" | custom-call | tf_op jit(solution)/shard_map/pallas_call | solution.py:293
  46.3 1.3 %copy.12 = f32[2,512]{1,0:T(2,128)} copy(f32[2,512]{1,0:T(2,128)} %shard_map.100) | data formatting | bytes 8192
where the time goes:
time: 47.7 us; the launch traced here: 47.6 us
  Pallas kernels  46.3 us (97%)
  local copies, waits for them, and re-layouts  1.28 us (3%)
    pallas_call x1, Pallas kernels, local(): pl.pallas_call(functools.partial(kernel, ns, nr, first_column), out_shape...  46.3 us
    unnamed x1, local copies, waits for them, and re-layouts  1.28 us

commit v1 on v0

--- a/solution.py
+++ b/solution.py
@@ -44,8 +44,8 @@
     excite, history, basis, directions, centers, counts, neighbours, near_hbm, inv_hbm, rad_hbm,
     out,
     rad, rh, rl, near, inv, window, cwindow, twice, weight, ochunk, y1, y2, e0, p2, got1, send2, got2, samp,
-    near1, near2, cur,
-    rad_sem, near_sem, inv_sem, win_s, win_r, s1, r1, s2, r2, s3, r3,
+    near1, near2, cur, wl, gotw,
+    rad_sem, near_sem, inv_sem, win_s, win_r, s1, r1, s2, r2, s3, r3, sw, rw,
 ):
     boxes, pb = near_hbm.shape[0], near_hbm.shape[-1]
     slots = near_hbm.shape[1]
@@ -133,12 +133,15 @@
     def scatter(src, t, i):
         return send(src.at[i], got1.at[t, i], s1.at[t, i], r1.at[t, i], (c, quarter(i)))
 
-    def translate(src, t, copies):
+    def reduce(src, t, copies):
         for copy in copies:
             copy.wait_recv()
         reduced = src[nr - 1]
         for i in range(nr - 1):
             reduced = reduced + got1[t, i]
+        return reduced
+
+    def translate(reduced, t):
         for s in range(ns):
             send2[t, s] = reduced[s : s + 1, :]
         return [
@@ -208,7 +211,8 @@
             here = pl.ds(pl.multiple_of(j * db, db), db)
             w, c2 = weight[i, :, here], twice[i, :, here]
             y2[i, :, here] = w * clenshaw(lambda m: p2[i, m : m + 1, here], c2, (ns, db))
-            e0[i, :, here] = w * clenshaw(lambda m: first_column[m], c2, (ns, db))
+            if i == nr - 1:
+                e0[:, here] = w * clenshaw(lambda m: first_column[m], c2, (ns, db))
 
     def near_part():
         near_load.wait()
@@ -229,13 +233,14 @@
             near1[b] = dot_nt(ones, now, EXACT)
             near2[b] = dot_nt(ones, later, EXACT)
 
+    copies = translate(reduce(y1, 0, copies), 0)
+    known = []
+    for i in range(nr):
+        later_part(i)
+        if i < nr - 1:
+            known.append(scatter(y2, 1, i))
     near_part()
-    copies = translate(y1, 0, copies)
-    for i in range(nr // 2):
-        later_part(i)
     copies = collect(0, copies)
-    for i in range(nr // 2, nr):
-        later_part(i)
     inv_load.wait()
     solve(0, copies, near1)
 
@@ -251,11 +256,17 @@
             here = pl.ds(pl.multiple_of(j * db, db), db)
             top = dot_nt(xc, rh[i, here, :])
             low = dot_nt(xc[:8], rl[i, here, :])
-            value = (top[:8] + top[8:] + low)[:1]
-            y2[i, :, here] = y2[i, :, here] + e0[i, :, here] * value
+            wl[i, :, here] = (top[:8] + top[8:] + low)[:1]
 
         if i < nr - 1:
-            copies.append(scatter(y2, 1, i))
+            copies.append(send(wl.at[i], gotw.at[i], sw.at[i], rw.at[i], (c, quarter(i))))
+    known = reduce(y2, 1, known)
+    for copy in copies:
+        copy.wait_recv()
+    fresh = wl[nr - 1]
+    for i in range(nr - 1):
+        fresh = fresh + gotw[i]
+    copies = translate(known + e0[...] * fresh, 1)
     for copy in win_copies:
         copy.wait_recv()
     ones = jnp.ones((8, pb), F32)
@@ -267,7 +278,6 @@
             now = now + near[b, j, 0] * cwindow[place(b, j)][:1]
         near2[b] = near2[b] + dot_nt(ones, now, EXACT)
 
-    copies = translate(y2, 1, copies)
     copies = collect(1, copies)
     solve(1, copies, near2)
     for copy in sent:
@@ -308,7 +318,7 @@
             pltpu.VMEM((TAU, db), F32),
             pltpu.VMEM((nr, ns, rq), F32),
             pltpu.VMEM((nr, ns, rq), F32),
-            pltpu.VMEM((nr, ns, rq), F32),
+            pltpu.VMEM((ns, rq), F32),
             pltpu.VMEM((nr, TAU, rq), F32),
             pltpu.VMEM((steps, nr - 1, ns, rq), F32),
             pltpu.VMEM((steps, ns, 1, rq), F32),
@@ -317,11 +327,14 @@
             pltpu.VMEM((boxes, 8, pb), F32),
             pltpu.VMEM((boxes, 8, pb), F32),
             pltpu.VMEM((boxes, 8, pb), F32),
+            pltpu.VMEM((nr, 1, rq), F32),
+            pltpu.VMEM((nr - 1, 1, rq), F32),
             dma((nr,)), dma(()), dma(()),
             dma((steps, 2)), dma((steps, 2)),
             dma((steps, nr - 1)), dma((steps, nr - 1)),
             dma((steps, ns - 1)), dma((steps, ns - 1)),
             dma((steps, nr - 1)), dma((steps, nr - 1)),
+            dma((nr - 1,)), dma((nr - 1,)),
         ],
         compiler_params=pltpu.CompilerParams(
             collective_id=0, has_side_effects=True, vmem_limit_bytes=58 * 1024 * 1024

time: 47.7 us -> 45.3 us (0.950)
  Pallas kernels: 46.3 us -> 43.8 us
    pallas_call x1, Pallas kernels: 46.3 us -> 43.8 us  [local(): pl.pallas_call(functools.partial(kernel, ns, nr, first_column), out_shape...]
where the time goes in v1:
time: 45.3 us; the launch traced here: 45.1 us
  Pallas kernels  43.8 us (97%)
  local copies, waits for them, and re-layouts  1.28 us (3%)
    pallas_call x1, Pallas kernels, local(): pl.pallas_call(functools.partial(kernel, ns, nr, first_column), out_shape...  43.8 us
    unnamed x1, local copies, waits for them, and re-layouts  1.28 us

profile of v1, /device:TPU:0, one launch (start us, length us, event | category | flops | bytes accessed | tf_op | source)
XLA Modules:
  0.0 45.1 jit_solution(16472268078660863415)
XLA Ops:
  0.0 43.8 %shard_map.100 = f32[2,512]{1,0:T(2,128)} custom-call(f32[2,512]{1,0:T(2,128)} %excite.1, f32[64,512]{1,0:T(8,128)} %history.1, f32[96,64]{1,0:T(8,128)} %constant.2.clone.basis, f32[3,8192]{1,0:T(4,128)} %directions.1, f32[3,8]{1,0:T(4,128)} %centers.1, s32[4]{0:T(128)} %counts.1, s32[4,8]{1,0:T(4,128)} %neighbours.1, f32[4,8,3,128,128]{4,3,2,1,0:T(8,128)} %near_hbm.1, ...), custom_call_target="tpu_custom_call" | custom-call | tf_op jit(solution)/shard_map/pallas_call | solution.py:303
  43.9 1.3 %copy.12 = f32[2,512]{1,0:T(2,128)} copy(f32[2,512]{1,0:T(2,128)} %shard_map.100) | data formatting | bytes 8192
